TPU v7x, 256 devices: a whole 4x4x8 slice. The times are simulated.
256 devices in a mesh: txt: 8 (over z), clip: 8 (over x, core), proj: 4 (over y).
Axes of the slice: x: 4, y: 4, z: 8, core: 2. Of those that a mesh axis runs over, the one named last changes fastest.
Arguments:
- text_hidden: float32 [8192, 1024], P(('txt', 'clip')), may hold values from -16 to 16
- proj_weight: float32 [1024, 1024], P(None, 'proj'), may hold values from -2 to 2
- clip_embed: float32 [8192, 1024], P(('txt', 'clip'), 'proj'), may hold values from -16 to 16
- positive: int32 [8192], P(('txt', 'clip')), may hold values from 0 to 8191, each once
- logit_scale: float32 [1], replicated, may hold values from 10 to 300
Outputs:
- grad_hidden: float32 [8192, 1024], P(('txt', 'clip'), 'proj')
- grad_weight: float32 [1024, 1024], P(('txt', 'clip'), 'proj')
- grad_clip: float32 [8192, 1024], P(('txt', 'clip'), 'proj')
Inputs may be any that keep to these rules, and one draw needn't show every extreme that they name: `positive`: each clip row is the match of exactly one text row.
All inputs are finite; a program needn't handle non-finite values.
Results may differ from a plain program's by a relative error of at most 0.0003.
Values sent between devices are 32-bit elements; how exact they have to be, the bound alone decides.
A program may use at most 64 MiB of HBM per device.

v0:
```python
import jax
import jax.numpy as jnp
from jax import lax
from jax.sharding import PartitionSpec as P

EPSILON = 1e-06
PRECISE = lax.Precision.HIGHEST


def in_order(blocks, dim):
    lengths = list(blocks.shape[1:])
    lengths[dim] *= blocks.shape[0]
    return jnp.moveaxis(blocks, 0, dim).reshape(lengths)


def sent_to_all(array, axis):
    size = lax.axis_size(axis)
    return lax.all_to_all(
        jnp.broadcast_to(array[None], (size, *array.shape)), axis, 0, 0, tiled=True
    )


def gather_directly(array, axis, dim):
    return in_order(sent_to_all(array, axis), dim)


def all_in_one(array, axis):
    leaves = jax.tree.leaves(array)
    order = sorted(range(len(leaves)), key=lambda k: -leaves[k].size)
    width = (1, *leaves[order[0]].shape)[-1]
    lines = [
        jnp.pad(leaves[k].reshape(-1), (0, -leaves[k].size % width)).reshape(-1, width)
        for k in order
    ]
    both, at, found = (sent_to_all(jnp.concatenate(lines), axis), 0, {})
    for k, line in zip(order, lines):
        section = both[:, at : at + len(line)].reshape(len(both), -1)
        found[k] = section[:, : leaves[k].size].reshape(-1, *leaves[k].shape)
        at += len(line)
    numbers = iter(range(len(leaves)))
    return jax.tree.map(lambda _: found[next(numbers)], array)


def combined_pairwise(pieces, combine):
    while len(jax.tree.leaves(pieces)[0]) > 1:
        pieces = jax.vmap(combine)(
            *(jax.tree.map(lambda part: part[side::2], pieces) for side in (0, 1))
        )
    return jax.tree.map(lambda part: part[0], pieces)


def combined_all(array, axis, combine):
    pieces = all_in_one(array, axis)
    return combined_pairwise(pieces, combine)


def cut_along(array, dim, size):
    lengths = array.shape
    blocks = array.reshape(*lengths[:dim], size, lengths[dim] // size, *lengths[dim + 1 :])
    return jnp.moveaxis(blocks, dim, 0)


def sent_and_summed(array, axis, dim):
    size = lax.axis_size(axis)
    blocks = lax.all_to_all(cut_along(array, dim, size), axis, 0, 0, tiled=True)
    return jnp.sum(blocks, axis=0)


def unit_rows(raw):
    inverse = lax.rsqrt(jnp.sum(raw * raw, axis=1, keepdims=True) + EPSILON)
    return (raw * inverse, inverse)


def unit_back(unit, inverse, upstream):
    along = jnp.sum(unit * upstream, axis=1, keepdims=True)
    return (upstream - unit * along) * inverse


def paired_stats(earlier, later):
    top = jnp.maximum(earlier[0], later[0])
    total = earlier[1] * jnp.exp(earlier[0] - top) + later[1] * jnp.exp(later[0] - top)
    return (top, total)


def body(text_hidden, proj_weight, clip_embed, positive, logit_scale):
    score_scale = logit_scale[0]
    clip_groups = lax.axis_size("clip")
    proj_groups = lax.axis_size("proj")
    sub_rows = text_hidden.shape[0]
    quarter = sub_rows // proj_groups
    projected = jnp.dot(
        text_hidden, proj_weight, precision=PRECISE, preferred_element_type=jnp.float32
    )
    text_rows, clip_rows = (
        lax.all_to_all(projected, "proj", split_axis=0, concat_axis=1, tiled=True),
        lax.all_to_all(clip_embed, "proj", split_axis=0, concat_axis=1, tiled=True),
    )
    text_unit, text_inverse = unit_rows(text_rows)
    clip_unit, clip_inverse = unit_rows(clip_rows)
    own_proj = lax.axis_index("proj")
    own_clip = lax.axis_index("clip")
    own_positive = lax.dynamic_slice_in_dim(positive, own_proj * quarter, quarter)
    clip_near = gather_directly(clip_unit, "txt", 0)
    text_tile, positive_tile = (
        lax.all_gather(text_unit, ("clip", "proj"), axis=0, tiled=True),
        lax.all_gather(own_positive, ("clip", "proj"), axis=0, tiled=True),
    )
    block_index = positive_tile // sub_rows
    remainder = positive_tile % sub_rows
    inside = (block_index % clip_groups == own_clip) & (remainder // quarter == own_proj)
    column = jnp.where(inside, block_index // clip_groups * quarter + remainder % quarter, -1)
    scores = score_scale * lax.dot_general(
        text_tile,
        clip_near,
        (((1,), (1,)), ((), ())),
        precision=PRECISE,
        preferred_element_type=jnp.float32,
    )
    local_row_max = jnp.max(scores, axis=1)
    local_col_max = jnp.max(scores, axis=0)
    row_local = (local_row_max, jnp.sum(jnp.exp(scores - local_row_max[:, None]), axis=1))
    row_max, row_total = combined_all(row_local, ("clip", "proj"), paired_stats)
    col_local = (local_col_max, jnp.sum(jnp.exp(scores - local_col_max[None, :]), axis=0))
    col_max, col_total = combined_all(col_local, "txt", paired_stats)
    row_exp = jnp.exp(scores - row_max[:, None])
    col_exp = jnp.exp(scores - col_max[None, :])
    matches = (lax.broadcasted_iota(jnp.int32, scores.shape, 1) == column[:, None]).astype(
        jnp.float32
    )
    grad_scores = 0.5 * (row_exp / row_total[:, None] + col_exp / col_total[None, :]) - matches
    text_cot = lax.psum_scatter(
        score_scale
        * jnp.dot(grad_scores, clip_near, precision=PRECISE, preferred_element_type=jnp.float32),
        ("clip", "proj"),
        scatter_dimension=0,
        tiled=True,
    )
    clip_cot = sent_and_summed(
        score_scale
        * lax.dot_general(
            grad_scores,
            text_tile,
            (((0,), (0,)), ((), ())),
            precision=PRECISE,
            preferred_element_type=jnp.float32,
        ),
        "txt",
        0,
    )
    text_back = unit_back(text_unit, text_inverse, text_cot)
    clip_back = unit_back(clip_unit, clip_inverse, clip_cot)
    text_cols, grad_clip = (
        lax.all_to_all(text_back, "proj", split_axis=1, concat_axis=0, tiled=True),
        lax.all_to_all(clip_back, "proj", split_axis=1, concat_axis=0, tiled=True),
    )
    grad_weight = sent_and_summed(
        lax.dot_general(
            text_hidden,
            text_cols,
            (((0,), (0,)), ((), ())),
            precision=PRECISE,
            preferred_element_type=jnp.float32,
        ),
        ("txt", "clip"),
        0,
    )
    partial_hidden = lax.dot_general(
        text_cols,
        proj_weight,
        (((1,), (1,)), ((), ())),
        precision=PRECISE,
        preferred_element_type=jnp.float32,
    )
    grad_hidden = sent_and_summed(partial_hidden, "proj", 1)
    return (grad_hidden, grad_weight, grad_clip)


def solution(mesh):
    in_specs = (
        P(("txt", "clip"), None),
        P(None, "proj"),
        P(("txt", "clip"), "proj"),
        P(("txt", "clip")),
        P(),
    )
    out_specs = (P(("txt", "clip"), "proj"), P(("txt", "clip"), "proj"), P(("txt", "clip"), "proj"))
    return jax.shard_map(body, mesh=mesh, in_specs=in_specs, out_specs=out_specs, check_vma=False)
```

profile of v0, /device:TPU:1, one launch (start us, length us, event | category | flops | bytes accessed | tf_op | source)
XLA Modules:
  0.0 288.7 jit_solution(14806833728530572804)
XLA Ops:
  7.2 1.1 copy-done
  8.4 1.7 fusion.19
  10.1 9.6 %all_to_all.103 = f32[4,32,256]{2,1,0:T(8,128)S(1)} all-to-all(f32[4,32,256]{2,1,0:T(8,128)S(1)} %bitcast.94), channel_id=1, replica_groups=mesh['txt'=8,'clip'=8,'proj'=4] {'proj'}, dimensions={0} | all-to-all | bytes 262144 | tf_op jit(solution)/shard_map/all_to_all | solution.py:95
  19.9 0.7 broadcast_multiply_fusion.1
  20.6 8.1 %all_to_all.104 = f32[4,32,256]{2,1,0:T(8,128)S(1)} all-to-all(f32[4,32,256]{2,1,0:T(8,128)} %bitcast.95), channel_id=1, replica_groups=mesh['txt'=8,'clip'=8,'proj'=4] {'proj'}, dimensions={0} | all-to-all | bytes 262144 | tf_op jit(solution)/shard_map/all_to_all | solution.py:96
  29.0 1.1 broadcast_in_dim.8
  30.1 8.2 %all-to-all-start.2 = ((f32[8,32,1024]{2,1,0:T(8,128)}), f32[8,32,1024]{2,1,0:T(8,128)S(1)}, u32[]{:S(2)}, u32[]{:S(2)}) async-start(f32[8,32,1024]{2,1,0:T(8,128)} %broadcast_in_dim.8), calls=%async_computation.2 | async-start | bytes 2097152 | tf_op jit(solution)/shard_map/all_to_all | solution.py:18
  40.4 17.2 %all-reduce = s32[1024]{0:T(1024)S(1)} all-reduce(s32[1024]{0:T(1024)S(1)} %dynamic-slice_dynamic-update-slice_fusion), channel_id=1, replica_groups=mesh['txt'=8,'clip'=8,'proj'=4] {'clip','proj'}, use_global_device_ids=true, to_apply=%add | all-reduce | flops 1024 | bytes 8192
  57.6 6.9 %all-to-all-done.2 = f32[8,32,1024]{2,1,0:T(8,128)S(1)} async-done(((f32[8,32,1024]{2,1,0:T(8,128)}), f32[8,32,1024]{2,1,0:T(8,128)S(1)}, u32[]{:S(2)}, u32[]{:S(2)}) %all-to-all-start.2) | async-done | bytes 1048608 | tf_op jit(solution)/shard_map/all_to_all | solution.py:18
  64.4 10.2 %all-gather.2.cloned.1.call-done = f32[1024,1024]{1,0:T(8,128)} async-done(((f32[32,1024]{1,0:T(8,128)}), f32[1024,1024]{1,0:T(8,128)}) %all-gather.2.cloned.1.call-update) | async-done | bytes 4194320 | tf_op jit(solution)/shard_map/all_gather | solution.py:105
  74.7 5.4 %fusion.16 = (f32[1024]{0:T(1024)S(1)}, f32[256]{0:T(256)S(1)}, f32[1024,256]{1,0:T(8,128)S(1)}) fusion(f32[1024,1024]{1,0:T(8,128)} %all-gather.2.cloned.1.call-done, f32[256,1024]{1,0:T(8,128)S(1)} %bitcast.79, f32[]{:T(128)} %bitcast.76), kind=kOutput, calls=%fused_computation.74 | convolution fusion | flops 3222010624 | bytes 6296580 | tf_op jit(solution)/shard_map/dot_general | solution.py:112
  81.2 6.7 %all-to-all-start.4 = ((f32[8,2,256]{2,1,0:T(2,128)}), f32[8,2,256]{2,1,0:T(2,128)S(1)}, u32[]{:S(2)}, u32[]{:S(2)}) async-start(f32[8,2,256]{2,1,0:T(2,128)} %broadcast_in_dim.10), calls=%async_computation.4 | async-start | bytes 32768 | tf_op jit(solution)/shard_map/all_to_all | solution.py:18
  87.9 6.6 %all-to-all-done.4 = f32[8,2,256]{2,1,0:T(2,128)S(1)} async-done(((f32[8,2,256]{2,1,0:T(2,128)}), f32[8,2,256]{2,1,0:T(2,128)S(1)}, u32[]{:S(2)}, u32[]{:S(2)}) %all-to-all-start.4) | async-done | bytes 16416 | tf_op jit(solution)/shard_map/all_to_all | solution.py:18
  94.5 0.8 broadcast_in_dim.9
  95.3 6.7 %all-to-all-start.3 = ((f32[32,2,1024]{2,1,0:T(2,128)}), f32[32,2,1024]{2,1,0:T(2,128)}, u32[]{:S(2)}, u32[]{:S(2)}) async-start(f32[32,2,1024]{2,1,0:T(2,128)} %broadcast_in_dim.9), calls=%async_computation.3 | async-start | bytes 524288 | tf_op jit(solution)/shard_map/all_to_all | solution.py:18
  103.1 7.8 %all-to-all-done.3 = f32[32,2,1024]{2,1,0:T(2,128)} async-done(((f32[32,2,1024]{2,1,0:T(2,128)}), f32[32,2,1024]{2,1,0:T(2,128)}, u32[]{:S(2)}, u32[]{:S(2)}) %all-to-all-start.3) | async-done | bytes 262176 | tf_op jit(solution)/shard_map/all_to_all | solution.py:18
  110.9 1.3 fusion.17
  112.1 0.7 copy_bitcast_fusion.1
  112.9 1.5 slice.118
  114.4 1.5 slice.117
  115.9 0.6 slice.129
  116.6 0.6 slice.128
  117.2 1.0 multiply_add_fusion
  118.2 0.6 slice.131
  119.5 0.8 multiply_add_fusion.1
  120.6 6.3 %convolution_multiply_fusion = f32[1024,1024]{1,0:T(8,128)} fusion(f32[256,1024]{1,0:T(8,128)S(1)} %bitcast.80, f32[]{:T(128)} %bitcast.75, f32[1024,256]{1,0:T(8,128)S(1)} %get-tuple-element.27, s32[1024]{0:T(1024)S(1)} %fusion.8, f32[256]{0:T(256)S(1)} %bitcast.104, f32[256]{0:T(256)} %bitcast.106, f32[1024]{0:T(1024)S(1)} %bitcast.99, f32[1024]{0:T(1024)S(1)} %bitcast.101), kind=kOutput, calls=%fused_computation | convolution fusion | flops 3224633344 | bytes 6305796 | tf_op jit(solution)/shard_map/dot_general | solution.py:133
  126.9 0.7 copy-done.2
  127.5 6.3 %convolution_multiply_fusion.1 = f32[256,1024]{1,0:T(8,128)S(1)} fusion(f32[1024,1024]{1,0:T(8,128)} %all-gather.2.cloned.1.call-done, f32[]{:T(128)} %bitcast.77, f32[1024,256]{1,0:T(8,128)S(1)} %get-tuple-element.27, s32[1024]{0:T(1024)S(1)} %fusion.8, f32[256]{0:T(256)S(1)} %bitcast.105, f32[256]{0:T(256)S(1)} %bitcast.107, f32[1024]{0:T(1024)S(1)} %bitcast.100, ...), kind=kOutput, calls=%fused_computation.1 | convolution fusion | flops 3223846912 | bytes 6305796 | tf_op jit(solution)/shard_map/dot_general | solution.py:140
  133.9 31.1 %all_to_all.105 = f32[8,32,1024]{2,1,0:T(8,128)S(1)} all-to-all(f32[8,32,1024]{2,1,0:T(8,128)S(1)} %bitcast.90), channel_id=1, replica_groups=mesh['txt'=8,'clip'=8,'proj'=4] {'txt'}, dimensions={0} | all-to-all | bytes 2097152 | tf_op jit(solution)/shard_map/all_to_all | solution.py:65
  165.3 42.5 %reduce-scatter.2.cloned.1.call-done = f32[32,1024]{1,0:T(8,128)} async-done(((f32[1024,1024]{1,0:T(8,128)}), f32[32,1024]{1,0:T(8,128)}) %reduce-scatter.2.cloned.1.call-update) | async-done | bytes 131088 | tf_op jit(solution)/shard_map/reduce_scatter | solution.py:131
  207.7 1.1 multiply_reduce_fusion
  208.8 1.0 subtract_multiply_fusion
  209.8 0.7 copy.48
  210.5 3.3 %all-to-all-start.5 = ((f32[32,4,256]{2,0,1:T(8,128)}), f32[32,4,256]{2,0,1:T(8,128)S(1)}, u32[]{:S(2)}, u32[]{:S(2)}) async-start(f32[32,4,256]{2,0,1:T(8,128)} %bitcast.74), calls=%async_computation.6 | async-start | bytes 262144 | tf_op jit(solution)/shard_map/all_to_all | solution.py:153
  213.8 0.7 fusion
  214.6 4.0 %all-to-all-done.5 = f32[32,4,256]{2,0,1:T(8,128)S(1)} async-done(((f32[32,4,256]{2,0,1:T(8,128)}), f32[32,4,256]{2,0,1:T(8,128)S(1)}, u32[]{:S(2)}, u32[]{:S(2)}) %all-to-all-start.5) | async-done | bytes 131104 | tf_op jit(solution)/shard_map/all_to_all | solution.py:153
  218.6 3.3 %all-to-all-start.9 = ((f32[32,4,256]{2,0,1:T(8,128)}), f32[32,4,256]{2,0,1:T(8,128)S(1)}, u32[]{:S(2)}, u32[]{:S(2)}) async-start(f32[32,4,256]{2,0,1:T(8,128)} %fusion), calls=%async_computation.10 | async-start | bytes 262144 | tf_op jit(solution)/shard_map/all_to_all | solution.py:154
  222.0 2.0 convolution_bitcast_fusion.1
  224.0 2.8 all-to-all-done.9
  226.8 3.5 %all-to-all-start.6 = ((f32[4,128,256]{2,1,0:T(8,128)}), f32[4,128,256]{2,1,0:T(8,128)S(1)}, u32[]{:S(2)}, u32[]{:S(2)}) async-start(f32[4,128,256]{2,1,0:T(8,128)} %convolution_bitcast_fusion.1), calls=%async_computation.7 | async-start | bytes 1048576 | tf_op jit(solution)/shard_map/all_to_all | solution.py:65
  230.2 1.0 convolution_bitcast_fusion
  231.3 1.3 copy.30
  232.6 4.5 %all-to-all-done.6 = f32[4,128,256]{2,1,0:T(8,128)S(1)} async-done(((f32[4,128,256]{2,1,0:T(8,128)}), f32[4,128,256]{2,1,0:T(8,128)S(1)}, u32[]{:S(2)}, u32[]{:S(2)}) %all-to-all-start.6) | async-done | bytes 524320 | tf_op jit(solution)/shard_map/all_to_all | solution.py:65
  237.1 15.4 %all-to-all-start.7 = ((f32[64,16,256]{2,1,0:T(8,128)}), f32[64,16,256]{2,1,0:T(8,128)S(1)}, u32[]{:S(2)}, u32[]{:S(2)}) async-start(f32[64,16,256]{2,1,0:T(8,128)} %bitcast.24), calls=%async_computation.8 | async-start | bytes 2097152 | tf_op jit(solution)/shard_map/all_to_all | solution.py:65
  252.5 0.7 reduce_sum.88
  253.2 27.3 %all-to-all-done.7 = f32[64,16,256]{2,1,0:T(8,128)S(1)} async-done(((f32[64,16,256]{2,1,0:T(8,128)}), f32[64,16,256]{2,1,0:T(8,128)S(1)}, u32[]{:S(2)}, u32[]{:S(2)}) %all-to-all-start.7) | async-done | bytes 1048608 | tf_op jit(solution)/shard_map/all_to_all | solution.py:65
  280.5 0.7 reduce_sum.89
  281.2 0.7 copy.52
  (56 shorter events, 4.5 us)
Async XLA Ops:
  7.2 1.2 copy-start
  7.2 31.7 %copy-start.4 = (u32[256]{0:T(256)S(1)}, u32[256]{0:T(256)}, u32[]{:S(2)}) copy-start(u32[256]{0:T(256)} %constant.89) | copy-start | bytes 3076
  7.2 33.0 %copy-start.3 = (s32[128]{0:T(128)S(1)}, s32[128]{0:T(128)}, u32[]{:S(2)}) copy-start(s32[128]{0:T(128)} %param.8) | copy-start | bytes 1540
  7.2 67.5 %all-gather.2.cloned.1.call-start = ((), (), s32[]{:S(2)}) async-start(), calls=%async_computation.11 | async-start | bytes 4325376 | tf_op jit(solution)/shard_map/all_gather | solution.py:105
  30.1 34.3 %all-to-all-start.2 = ((f32[8,32,1024]{2,1,0:T(8,128)}), f32[8,32,1024]{2,1,0:T(8,128)S(1)}, u32[]{:S(2)}, u32[]{:S(2)}) async-start(f32[8,32,1024]{2,1,0:T(8,128)} %broadcast_in_dim.8), calls=%async_computation.2 | async-start | bytes 2097152 | tf_op jit(solution)/shard_map/all_to_all | solution.py:18
  81.2 13.4 %all-to-all-start.4 = ((f32[8,2,256]{2,1,0:T(2,128)}), f32[8,2,256]{2,1,0:T(2,128)S(1)}, u32[]{:S(2)}, u32[]{:S(2)}) async-start(f32[8,2,256]{2,1,0:T(2,128)} %broadcast_in_dim.10), calls=%async_computation.4 | async-start | bytes 32768 | tf_op jit(solution)/shard_map/all_to_all | solution.py:18
  95.3 15.6 %all-to-all-start.3 = ((f32[32,2,1024]{2,1,0:T(2,128)}), f32[32,2,1024]{2,1,0:T(2,128)}, u32[]{:S(2)}, u32[]{:S(2)}) async-start(f32[32,2,1024]{2,1,0:T(2,128)} %broadcast_in_dim.9), calls=%async_computation.3 | async-start | bytes 524288 | tf_op jit(solution)/shard_map/all_to_all | solution.py:18
  102.0 105.7 %reduce-scatter.2.cloned.1.call-start = ((), (), s32[]{:S(2)}) async-start(), calls=%async_computation.12 | async-start | bytes 4325376 | tf_op jit(solution)/shard_map/reduce_scatter | solution.py:131
  126.8 0.7 copy-start.2
  133.9 96.4 %copy-start.1 = (f32[128,1024]{1,0:T(8,128)S(1)}, f32[128,1024]{1,0:T(8,128)}, u32[]{:S(2)}) copy-start(f32[128,1024]{1,0:T(8,128)} %param.5) | copy-start | bytes 1572868
  210.5 8.1 %all-to-all-start.5 = ((f32[32,4,256]{2,0,1:T(8,128)}), f32[32,4,256]{2,0,1:T(8,128)S(1)}, u32[]{:S(2)}, u32[]{:S(2)}) async-start(f32[32,4,256]{2,0,1:T(8,128)} %bitcast.74), calls=%async_computation.6 | async-start | bytes 262144 | tf_op jit(solution)/shard_map/all_to_all | solution.py:153
  218.6 8.1 %all-to-all-start.9 = ((f32[32,4,256]{2,0,1:T(8,128)}), f32[32,4,256]{2,0,1:T(8,128)S(1)}, u32[]{:S(2)}, u32[]{:S(2)}) async-start(f32[32,4,256]{2,0,1:T(8,128)} %fusion), calls=%async_computation.10 | async-start | bytes 262144 | tf_op jit(solution)/shard_map/all_to_all | solution.py:154
  226.8 10.4 %all-to-all-start.6 = ((f32[4,128,256]{2,1,0:T(8,128)}), f32[4,128,256]{2,1,0:T(8,128)S(1)}, u32[]{:S(2)}, u32[]{:S(2)}) async-start(f32[4,128,256]{2,1,0:T(8,128)} %convolution_bitcast_fusion.1), calls=%async_computation.7 | async-start | bytes 1048576 | tf_op jit(solution)/shard_map/all_to_all | solution.py:65
  237.1 43.4 %all-to-all-start.7 = ((f32[64,16,256]{2,1,0:T(8,128)}), f32[64,16,256]{2,1,0:T(8,128)S(1)}, u32[]{:S(2)}, u32[]{:S(2)}) async-start(f32[64,16,256]{2,1,0:T(8,128)} %bitcast.24), calls=%async_computation.8 | async-start | bytes 2097152 | tf_op jit(solution)/shard_map/all_to_all | solution.py:65
Sparse Core Ops, SparseCore 0:
  20.8 53.8 all-gather.1
  127.0 80.7 reduce-scatter.1
where the time goes:
time: 290 us; the launch traced here: 289 us
  waiting for transfers between devices  113 us (39%)
  blocking collectives  66.1 us (23%)
  starting transfers between devices  47.4 us (16%)
  matrix products  22.7 us (8%)
  local copies, waits for them, and re-layouts  15.8 us (5%)
  between operations  15.6 us (5%)
  other arithmetic  8.45 us (3%)
    reduce_scatter x1, waiting for transfers between devices, body(): lax.psum_scatter(score_scale * jnp.dot(grad_scores, clip_near, precision=...  42.5 us
    all_to_all x2, waiting for transfers between devices, sent_and_summed(): blocks = lax.all_to_all(cut_along(array, dim, size), axis, 0, 0, tiled=True)  31.8 us
    all_to_all x1, blocking collectives, sent_and_summed(): blocks = lax.all_to_all(cut_along(array, dim, size), axis, 0, 0, tiled=True)  31.1 us
    all_to_all x3, starting transfers between devices, sent_to_all(): lax.all_to_all(jnp.broadcast_to(array[None], (size, *array.shape)), axis,...  21.7 us
    all_to_all x3, waiting for transfers between devices, sent_to_all(): lax.all_to_all(jnp.broadcast_to(array[None], (size, *array.shape)), axis,...  21.3 us
    all_to_all x2, starting transfers between devices, sent_and_summed(): blocks = lax.all_to_all(cut_along(array, dim, size), axis, 0, 0, tiled=True)  18.8 us
    unnamed x1, blocking collectives  17.2 us
    all_gather x1, waiting for transfers between devices, body(): lax.all_gather(text_unit, ('clip', 'proj'), axis=0, tiled=True)  10.2 us
  transfers between devices with their start and end apart: 9, of which 9 were waited for; matrix products, arithmetic and copies ran while one was open for 5% of the time, Pallas kernels for 0%

commit v1 on v0

v1 whole, which is shorter than its diff:
```python
import jax
import jax.numpy as jnp
from jax import lax
from jax.experimental import pallas as pl
from jax.experimental.pallas import tpu as pltpu
from jax.sharding import PartitionSpec as P

MESH = pl.DeviceIdType.MESH
EPSILON = 1e-06
PRECISE = lax.Precision.HIGHEST
F32 = jnp.float32
BF16 = jnp.bfloat16

NAMES = {}
COUNT = 0
for _name, _n in (
    ("clip_y", 3), ("pos_x", 3), ("pos_c", 1), ("a1", 3), ("b1", 3), ("a2", 12), ("b2", 12),
    ("pa", 4), ("pb", 4), ("gz", 16), ("stat_c", 1), ("stat_y", 3), ("stat_x", 3), ("stat_z", 7),
    ("rc", 4), ("xa", 3), ("yb", 3), ("ya", 3), ("xb", 3), ("cz", 16), ("hid", 3), ("wc", 1),
    ("wx", 3), ("wz", 7), ("gc", 3),
):
    NAMES[_name] = COUNT
    COUNT += _n


def split(value):
    high = value.astype(BF16)
    return high, (value - high.astype(F32)).astype(BF16)


def product(a, b, dims):
    return lax.dot_general(a, b, (dims, ((), ())), preferred_element_type=F32)


def product3(a, b, dims):
    (ah, al), (bh, bl) = a, b
    return product(ah, bh, dims) + product(ah, bl, dims) + product(al, bh, dims)


def exact(a, b, dims):
    return lax.dot_general(a, b, (dims, ((), ())), precision=PRECISE, preferred_element_type=F32)


def turned(column):
    return jnp.broadcast_to(column, (128, 128)).T[0:1, :]


def upright(line):
    return jnp.broadcast_to(line, (128, 128)).T[:, 0:1]


def joined(stats):
    top = stats[0][0]
    for part in stats[1:]:
        top = jnp.maximum(top, part[0])
    total = stats[0][1] * jnp.exp(stats[0][0] - top)
    for part in stats[1:]:
        total = total + part[1] * jnp.exp(part[0] - top)
    return top, total


def kernel(
    hid_ref, w_ref, clip_ref, pos_ref, scale_ref,
    gh_ref, gw_ref, gc_ref,
    text, text_h, text_l, clip, clip_h, clip_l, pos, inv_t, scores, exp_r, exp_c, max_t, sum_t,
    row_stat, row_got_c, row_got_y, row_got_x, col_stat, col_got, col_keep, fac_t, g_h, g_l,
    part, part_c, got_xa, got_yb, got_ya, got_xb, cpart, cgot, hpart, hgot, wpart, wgot_c, wgot_x, wgot_z,
    cback, ss, rs,
):
    z = lax.axis_index("txt")
    k = lax.axis_index("clip")
    y = lax.axis_index("proj")
    x = k // 2
    c = lax.rem(k, 2)
    o = 1 - c

    def on_z(d):
        return lax.rem(z + d, 8)

    def on_x(d):
        return lax.rem(x + d, 4)

    def on_y(d):
        return lax.rem(y + d, 4)

    partner = (z, 2 * x + o, y)

    def z_peer(d):
        return (on_z(d), k, y)

    def x_peer(d):
        return (z, 2 * on_x(d) + c, y)

    def y_peer(d):
        return (z, k, on_y(d))

    sent = []

    def copy_of(src, dst, slot, device):
        return pltpu.make_async_remote_copy(
            src_ref=src, dst_ref=dst, send_sem=ss.at[slot], recv_sem=rs.at[slot],
            device_id=device, device_id_type=MESH,
        )

    def send(src, dst, name, at, device):
        copy = copy_of(src, dst, NAMES[name] + at, device)
        copy.start()
        sent.append(copy)

    def arrived(place, name, at):
        copy_of(place, place, NAMES[name] + at, partner).wait_recv()

    peers = [partner] + [y_peer(d) for d in (1, 2, 3)] + [x_peer(d) for d in (1, 2, 3)]
    peers += [z_peer(d) for d in range(1, 8)]
    barrier = pltpu.get_barrier_semaphore()
    for device in peers:
        pl.semaphore_signal(barrier, inc=1, device_id=device, device_id_type=MESH)
    pl.semaphore_wait(barrier, len(peers))
    scale = scale_ref[0]

    for d in (1, 2, 3):
        rows = pl.ds(pl.multiple_of(on_y(d) * 32, 32), 32)
        send(clip_ref.at[rows], clip.at[z, y], "clip_y", d - 1, y_peer(d))
    pos[c, x] = jnp.broadcast_to(pos_ref[...], (8, 128))
    for d in (1, 2, 3):
        send(pos.at[c, x], pos.at[c, x], "pos_x", d - 1, x_peer(d))
    clip[z, y] = clip_ref[pl.ds(pl.multiple_of(y * 32, 32), 32), :]

    A, B = pl.ds(0, 64), pl.ds(64, 64)
    text[y, x, c, 0:64] = exact(hid_ref[0:64, :], w_ref[...], ((1,), (0,)))
    for d in (1, 3, 2):
        send(text.at[y, x, c, A], text.at[y, x, c, A], "a1", d - 1, x_peer(d))
    text[y, x, c, 64:128] = exact(hid_ref[64:128, :], w_ref[...], ((1,), (0,)))
    for d in (1, 3, 2):
        send(text.at[y, x, c, B], text.at[y, x, c, B], "b1", d - 1, y_peer(d))

    def forward_a(e):
        block = text.at[y, on_x(4 - e), c, A]
        for d in (1, 3, 2):
            send(block, block, "a2", e * 3 + d - 1, y_peer(d))

    def forward_b(e):
        block = text.at[on_y(4 - e), x, c, B]
        for d in (1, 3, 2):
            send(block, block, "b2", e * 3 + d - 1, x_peer(d))

    def ring_clip(step):
        for h in (0, 1):
            half = pl.ds(2 * h, 2)
            for way in (0, 1):
                if step > 1:
                    ring_clip_wait(step - 1, h, way)
                if step < 4 or h == way:
                    block = clip.at[on_z(9 - step) if way == 0 else on_z(step - 1), half]
                    send(block, block, "gz", way * 8 + (step - 1) * 2 + h, z_peer(1 if way == 0 else 7))

    def ring_clip_wait(step, h, way):
        block = clip.at[on_z(8 - step) if way == 0 else on_z(step), pl.ds(2 * h, 2)]
        arrived(block, "gz", way * 8 + (step - 1) * 2 + h)

    for d in (1, 2, 3):
        arrived(clip.at[z, on_y(4 - d)], "clip_y", d - 1)
    ring_clip(1)
    forward_a(0)
    forward_b(0)
    for d in (1, 2, 3):
        arrived(pos.at[c, on_x(4 - d)], "pos_x", d - 1)
    send(pos.at[c], pos.at[c], "pos_c", 0, partner)
    for e in (1, 3, 2):
        arrived(text.at[y, on_x(4 - e), c, A], "a1", e - 1)
        forward_a(e)
        arrived(text.at[on_y(4 - e), x, c, B], "b1", e - 1)
        forward_b(e)
    ring_clip(2)
    send(text.at[y, :, c, A], text.at[y, :, c, A], "pa", 0, partner)
    send(text.at[:, x, c, B], text.at[:, x, c, B], "pb", 0, partner)
    ring_clip(3)
    ring_clip(4)
    for d in (1, 3, 2):
        for e in (0, 1, 2, 3):
            arrived(text.at[on_y(4 - d), on_x(4 - e), c, A], "a2", e * 3 + d - 1)
        group = text.at[on_y(4 - d), :, c, A]
        send(group, group, "pa", d, partner)
        for e in (0, 1, 2, 3):
            arrived(text.at[on_y(4 - e), on_x(4 - d), c, B], "b2", e * 3 + d - 1)
        group = text.at[:, on_x(4 - d), c, B]
        send(group, group, "pb", d, partner)
    ring_clip_wait(4, 0, 0)
    ring_clip_wait(4, 1, 1)

    def clip_block(f, squares):
        block = clip[:, f].reshape(256, 256)
        clip_h[f], clip_l[f] = split(block)
        return squares + jnp.sum(block * block, axis=1, keepdims=True)

    inv_c = lax.rsqrt(lax.fori_loop(0, 4, clip_block, jnp.zeros((256, 1), F32)) + EPSILON)
    col_scale = scale * inv_c

    for d in (0, 1, 3, 2):
        arrived(text.at[on_y(4 - d), :, o, A], "pa", d)
        arrived(text.at[:, on_x(4 - d), o, B], "pb", d)
    arrived(pos.at[o], "pos_c", 0)

    def score(q, carry):
        squares = jnp.zeros((256, 1), F32)
        total = jnp.zeros((256, 256), F32)
        for f in range(4):
            block = text[f, q].reshape(256, 256)
            high, low = split(block)
            text_h[f, q], text_l[f, q] = high, low
            squares = squares + jnp.sum(block * block, axis=1, keepdims=True)
            total = total + product3((clip_h[f], clip_l[f]), (high, low), ((1,), (1,)))
        inverse = lax.rsqrt(squares + EPSILON)
        lanes = jnp.concatenate([turned(inverse[0:128]), turned(inverse[128:256])], axis=1)
        inv_t[q] = jnp.broadcast_to(lanes, (8, 256))
        tile = total * col_scale * lanes
        scores[q] = tile
        top = jnp.max(tile, axis=0, keepdims=True)
        raised = jnp.exp(tile - top)
        exp_r[q] = raised
        max_t[q] = jnp.broadcast_to(top, (8, 256))
        sum_t[q] = jnp.broadcast_to(jnp.sum(raised, axis=0, keepdims=True), (8, 256))
        return carry

    lax.fori_loop(0, 4, score, 0)

    for q in range(4):
        for h in (0, 1):
            row = 2 * q + h
            row_stat[0, row : row + 1, :] = max_t[q, 0:1, h * 128 : h * 128 + 128]
            row_stat[0, 8 + row : 9 + row, :] = sum_t[q, 0:1, h * 128 : h * 128 + 128]
    send(row_stat.at[0], row_got_c, "stat_c", 0, partner)
    top_c = jnp.max(scores[0], axis=1, keepdims=True)
    for q in range(1, 4):
        top_c = jnp.maximum(top_c, jnp.max(scores[q], axis=1, keepdims=True))
    total_c = jnp.zeros((256, 1), F32)
    for q in range(4):
        raised = jnp.exp(scores[q] - top_c)
        exp_c[q] = raised
        total_c = total_c + jnp.sum(raised, axis=1, keepdims=True)
    for h in (0, 1):
        col_stat[h : h + 1, :] = turned(top_c[h * 128 : h * 128 + 128])
        col_stat[2 + h : 3 + h, :] = turned(total_c[h * 128 : h * 128 + 128])
    col_stat[4:8, :] = jnp.zeros((4, 128), F32)
    for d in range(1, 8):
        send(col_stat, col_got.at[d - 1], "stat_z", d - 1, z_peer(d))

    def row_part(value):
        return value[0:8], value[8:16]

    arrived(row_got_c, "stat_c", 0)
    stats = joined([row_part(row_stat[0]), row_part(row_got_c[...])])
    row_stat[1, 0:8], row_stat[1, 8:16] = stats
    for d in (1, 3, 2):
        send(row_stat.at[1], row_got_y.at[d - 1], "stat_y", d - 1, y_peer(d))
    for d in (1, 2, 3):
        arrived(row_got_y.at[d - 1], "stat_y", d - 1)
    stats = joined([stats] + [row_part(row_got_y[d]) for d in range(3)])
    row_stat[2, 0:8], row_stat[2, 8:16] = stats
    for d in (1, 3, 2):
        send(row_stat.at[2], row_got_x.at[d - 1], "stat_x", d - 1, x_peer(d))
    for d in range(1, 8):
        arrived(col_got.at[d - 1], "stat_z", d - 1)

    def col_part(value):
        return value[0:2], value[2:4]

    top_g, total_g = joined([col_part(col_stat[...])] + [col_part(col_got[d]) for d in range(7)])
    fac = 0.5 * jnp.exp(col_stat[0:2] - top_g) / total_g
    fac_c = jnp.concatenate([upright(fac[0:1]), upright(fac[1:2])], axis=0)
    for d in (1, 2, 3):
        arrived(row_got_x.at[d - 1], "stat_x", d - 1)
    top_g, total_g = joined([stats] + [row_part(row_got_x[d]) for d in range(3)])
    fac = 0.5 * jnp.exp(row_stat[0, 0:8] - top_g) / total_g
    for q in range(4):
        for h in (0, 1):
            row = 2 * q + h
            fac_t[q, :, h * 128 : h * 128 + 128] = jnp.broadcast_to(fac[row : row + 1], (8, 128))

    number = lax.broadcasted_iota(jnp.int32, (256, 256), 0)
    clip_id = lax.shift_right_logical(number, 5) * 1024 + (number & 31) + (k * 128 + y * 32)

    def gradient(q, carry):
        target = jnp.concatenate([pos[0, q, 0:1, :], pos[1, q, 0:1, :]], axis=1)
        grad = exp_r[q] * fac_t[q, 0:1, :] + exp_c[q] * fac_c
        grad = grad - (clip_id == target).astype(F32)
        along = jnp.sum(grad * scores[q], axis=0, keepdims=True)
        g_h[q], g_l[q] = split(grad * (scale * inv_t[q, 0:1, :]))
        weighted = split(grad * col_scale)
        for f in range(4):
            block = product3(weighted, (clip_h[f], clip_l[f]), ((0,), (0,)))
            part[f, q, :, 8:136] = block.reshape(2, 128, 256)
            for h in (0, 1):
                line = jnp.broadcast_to(along[:, h * 128 : h * 128 + 128], (8, 128))
                part[f, q, h, 0:8] = jnp.concatenate([line, line], axis=1)
        copy_of(part.at[:, q, o], part_c.at[:, q], NAMES["rc"] + q, partner).start()
        return carry

    lax.fori_loop(0, 4, gradient, 0)
    for q in range(4):
        sent.append(copy_of(part.at[:, q, o], part_c.at[:, q], NAMES["rc"] + q, partner))

    def clip_gradient(f, carry):
        total = jnp.zeros((256, 256), F32)
        for q in range(4):
            total = total + product3((g_h[q], g_l[q]), (text_h[f, q], text_l[f, q]), ((1,), (0,)))
        cpart[:, f] = total.reshape(8, 32, 256)
        return carry

    lax.fori_loop(0, 4, clip_gradient, 0)

    def ring_sum(step):
        for h in (0, 1):
            half = pl.ds(2 * h, 2)
            for way in (0, 1):
                goal = on_z(5 - step) if way == 0 else on_z(3 + step)
                if step > 2 or (step == 2 and h == way):
                    place = cgot.at[way, step - 2, h]
                    arrived(place, "cz", way * 8 + (step - 2) * 2 + h)
                    cpart[goal, half] = cpart[goal, half] + place[...]
                if step > 1 or h == way:
                    send(
                        cpart.at[goal, half], cgot.at[way, step - 1, h],
                        "cz", way * 8 + (step - 1) * 2 + h, z_peer(1 if way == 0 else 7),
                    )

    ring_sum(1)
    for q in range(4):
        arrived(part_c.at[:, q], "rc", q)

    def add_core(q, carry):
        for f in range(4):
            part[f, q, c] = part[f, q, c] + part_c[f, q]
        return carry

    lax.fori_loop(0, 4, add_core, 0)
    first, second = pl.ds(0, 72), pl.ds(72, 64)
    for d in (1, 3, 2):
        send(part.at[:, on_x(d), c, first], got_xa.at[d - 1], "xa", d - 1, x_peer(d))
        send(part.at[on_y(d), :, c, second], got_yb.at[d - 1], "yb", d - 1, y_peer(d))
    ring_sum(2)
    ring_sum(3)
    ring_sum(4)
    for d in (1, 3, 2):
        arrived(got_xa.at[d - 1], "xa", d - 1)
        arrived(got_yb.at[d - 1], "yb", d - 1)

    def add_first(e, carry):
        part[e, x, c, 0:72] = part[e, x, c, 0:72] + got_xa[0, e] + got_xa[1, e] + got_xa[2, e]
        part[y, e, c, 72:136] = part[y, e, c, 72:136] + got_yb[0, e] + got_yb[1, e] + got_yb[2, e]
        return carry

    lax.fori_loop(0, 4, add_first, 0)
    for d in (1, 3, 2):
        send(part.at[on_y(d), x, c, first], got_ya.at[d - 1], "ya", d - 1, y_peer(d))
        send(part.at[y, on_x(d), c, second], got_xb.at[d - 1], "xb", d - 1, x_peer(d))

    for way in (0, 1):
        for h in (0, 1):
            arrived(cgot.at[way, 3, h], "cz", way * 8 + 6 + h)
    squares = jnp.zeros((32, 1), F32)
    along = jnp.zeros((32, 1), F32)
    for f in range(4):
        total = cpart[z, f] + cgot[0, 3, f // 2, f % 2] + cgot[1, 3, f // 2, f % 2]
        raw = clip[z, f]
        cback[f] = total
        squares = squares + jnp.sum(raw * raw, axis=1, keepdims=True)
        along = along + jnp.sum(raw * total, axis=1, keepdims=True)
    inverse = lax.rsqrt(squares + EPSILON)
    for f in range(4):
        cback[f] = (cback[f] - (clip[z, f] * inverse) * (along * inverse)) * inverse
    for d in (1, 3, 2):
        send(cback.at[on_y(d)], col_keep.at[d - 1], "gc", d - 1, y_peer(d))

    squares = jnp.zeros((128, 1), F32)
    for f in range(4):
        raw = text[f, x, c]
        squares = squares + jnp.sum(raw * raw, axis=1, keepdims=True)
    inverse = lax.rsqrt(squares + EPSILON)
    for d in (1, 3, 2):
        arrived(got_ya.at[d - 1], "ya", d - 1)
        arrived(got_xb.at[d - 1], "xb", d - 1)
    upper = part[y, x, c, 0:72] + got_ya[0] + got_ya[1] + got_ya[2]
    lower = part[y, x, c, 72:136] + got_xb[0] + got_xb[1] + got_xb[2]
    along = upright(upper[0:1, 0:128])
    cot = jnp.concatenate([upper[8:72], lower], axis=0)
    back = (cot - (text[y, x, c] * inverse) * along) * inverse

    for e in range(4):
        rows = slice(256 * e, 256 * e + 256)
        block = exact(hid_ref[:, rows], back, ((0,), (0,)))
        wpart[2 * e : 2 * e + 2] = block.reshape(2, 4, 2, 16, 256)
    send(wpart.at[:, :, o], wgot_c, "wc", 0, partner)
    for d in (2, 1, 3):
        rows = pl.ds(pl.multiple_of(on_y(d) * 256, 256), 256)
        hpart[d] = exact(back, w_ref[rows, :], ((1,), (1,)))
        send(hpart.at[d], hgot.at[d - 1], "hid", d - 1, y_peer(d))
    arrived(wgot_c, "wc", 0)

    def add_weight(e, carry):
        for f in range(4):
            wpart[e, f, c] = wpart[e, f, c] + wgot_c[e, f]
        return carry

    lax.fori_loop(0, 8, add_weight, 0)
    for d in (2, 1, 3):
        send(wpart.at[:, on_x(d), c], wgot_x.at[d - 1], "wx", d - 1, x_peer(d))
    own = exact(back, w_ref[pl.ds(pl.multiple_of(y * 256, 256), 256), :], ((1,), (1,)))
    for d in (1, 3, 2):
        arrived(wgot_x.at[d - 1], "wx", d - 1)
    wpart[:, x, c] = wpart[:, x, c] + wgot_x[0] + wgot_x[1] + wgot_x[2]
    for d in (4, 3, 5, 2, 6, 1, 7):
        send(wpart.at[on_z(d), x, c], wgot_z.at[d - 1], "wz", d - 1, z_peer(d))
    gc_ref[pl.ds(pl.multiple_of(y * 32, 32), 32), :] = cback[y]
    for d in (1, 2, 3):
        arrived(col_keep.at[d - 1], "gc", d - 1)
        gc_ref[pl.ds(pl.multiple_of(on_y(4 - d) * 32, 32), 32), :] = col_keep[d - 1]
    for d in (1, 3, 2):
        arrived(hgot.at[d - 1], "hid", d - 1)
    gh_ref[...] = own + hgot[0] + hgot[1] + hgot[2]
    total = wpart[z, x, c]
    for d in (1, 7, 2, 6, 3, 5, 4):
        arrived(wgot_z.at[d - 1], "wz", d - 1)
        total = total + wgot_z[d - 1]
    gw_ref[...] = total
    for copy in sent:
        copy.wait_send()


def body(text_hidden, proj_weight, clip_embed, positive, logit_scale):
    vmem = pl.BlockSpec(memory_space=pltpu.VMEM)
    scratch = [
        ((4, 4, 2, 128, 256), F32), ((4, 4, 256, 256), BF16), ((4, 4, 256, 256), BF16),
        ((8, 4, 32, 256), F32), ((4, 256, 256), BF16), ((4, 256, 256), BF16),
        ((2, 4, 8, 128), jnp.int32), ((4, 8, 256), F32),
        ((4, 256, 256), F32), ((4, 256, 256), F32), ((4, 256, 256), F32), ((4, 8, 256), F32), ((4, 8, 256), F32),
        ((3, 16, 128), F32), ((16, 128), F32), ((3, 16, 128), F32), ((3, 16, 128), F32),
        ((8, 128), F32), ((7, 8, 128), F32), ((3, 32, 256), F32), ((4, 8, 256), F32),
        ((4, 256, 256), BF16), ((4, 256, 256), BF16),
        ((4, 4, 2, 136, 256), F32), ((4, 4, 136, 256), F32),
        ((3, 4, 72, 256), F32), ((3, 4, 64, 256), F32), ((3, 72, 256), F32), ((3, 64, 256), F32),
        ((8, 4, 32, 256), F32), ((2, 4, 2, 2, 32, 256), F32),
        ((4, 128, 256), F32), ((3, 128, 256), F32),
        ((8, 4, 2, 16, 256), F32), ((8, 4, 16, 256), F32), ((3, 8, 16, 256), F32), ((7, 16, 256), F32),
        ((4, 32, 256), F32),
    ]
    return pl.pallas_call(
        kernel,
        out_shape=(
            jax.ShapeDtypeStruct((128, 256), F32),
            jax.ShapeDtypeStruct((16, 256), F32),
            jax.ShapeDtypeStruct((128, 256), F32),
        ),
        in_specs=[vmem, vmem, vmem, vmem, pl.BlockSpec(memory_space=pltpu.SMEM)],
        out_specs=(vmem, vmem, vmem),
        scratch_shapes=[pltpu.VMEM(shape, dtype) for shape, dtype in scratch]
        + [pltpu.SemaphoreType.DMA((COUNT,)), pltpu.SemaphoreType.DMA((COUNT,))],
        compiler_params=pltpu.CompilerParams(
            collective_id=0, has_side_effects=True, vmem_limit_bytes=56 << 20
        ),
        name="contrastive",
    )(text_hidden, proj_weight, clip_embed, positive.reshape(1, 128), logit_scale)


def solution(mesh):
    rows = ("txt", "clip")
    in_specs = (P(rows, None), P(None, "proj"), P(rows, "proj"), P(rows), P())
    out_specs = (P(rows, "proj"), P(rows, "proj"), P(rows, "proj"))
    return jax.shard_map(body, mesh=mesh, in_specs=in_specs, out_specs=out_specs, check_vma=False)
```

time: 290 us -> 92.8 us (0.32)
  waiting for transfers between devices: 113 us -> 0 us
  Pallas kernels: 0 us -> 88.4 us
  blocking collectives: 66.1 us -> 0 us
  starting transfers between devices: 47.4 us -> 0 us
  matrix products: 22.7 us -> 0 us
  between operations: 15.6 us -> 1.3 us
  local copies, waits for them, and re-layouts: 15.8 us -> 2.87 us
  other arithmetic: 8.45 us -> 0 us
    pallas_call x0 -> x1, Pallas kernels: none -> 88.4 us  [body(): pl.pallas_call(kernel, out_shape=(jax.ShapeDtypeStruct((128, 256), F32),...]
    all_to_all x7 -> x0, waiting for transfers between devices: 59.9 us -> none  [the longest x2 31.8 us: sent_and_summed(): blocks = lax.all_to_all(cut_along(array, dim, size), axis, 0, 0, tiled=True)]
    all_to_all x3 -> x0, blocking collectives: 48.9 us -> none  [the longest x1 31.1 us: sent_and_summed(): blocks = lax.all_to_all(cut_along(array, dim, size), axis, 0, 0, tiled=True)]
    all_to_all x7 -> x0, starting transfers between devices: 47.2 us -> none  [the longest x3 21.7 us: sent_to_all(): lax.all_to_all(jnp.broadcast_to(array[None], (size, *array.shape)), axis,...]
    reduce_scatter x1 -> x0, waiting for transfers between devices: 42.5 us -> none  [body(): lax.psum_scatter(score_scale * jnp.dot(grad_scores, clip_near, precision=...]
    dot_general x6 -> x0, matrix products: 22.7 us -> none  [the longest x1 6.32 us: body(): lax.dot_general(grad_scores, text_tile, (((0,), (0,)), ((), ())), precisi...]
    unnamed x1 -> x0, blocking collectives: 17.2 us -> none
    all_gather x1 -> x0, waiting for transfers between devices: 10.2 us -> none  [body(): lax.all_gather(text_unit, ('clip', 'proj'), axis=0, tiled=True)]
  transfers between devices with their start and end apart: 9 -> 0, of which waited for: 9 -> 0; matrix products, arithmetic and copies ran while one was open for 5% -> 0% of each run, Pallas kernels for 0% -> 0%
where the time goes in v1:
time: 92.8 us; the launch traced here: 92.6 us
  Pallas kernels  88.4 us (95%)
  local copies, waits for them, and re-layouts  2.87 us (3%)
  between operations  1.3 us (1%)
    pallas_call x1, Pallas kernels, body(): pl.pallas_call(kernel, out_shape=(jax.ShapeDtypeStruct((128, 256), F32),...  88.4 us
    unnamed x7, local copies, waits for them, and re-layouts  2.87 us

profile of v1, /device:TPU:1, one launch (start us, length us, event | category | flops | bytes accessed | tf_op | source)
XLA Modules:
  0.0 92.6 jit_solution(12196706279450342576)
XLA Ops:
  1.3 88.4 %contrastive.1 = (f32[128,256]{1,0:T(8,128)}, f32[16,256]{1,0:T(8,128)}, f32[128,256]{1,0:T(8,128)}) custom-call(f32[128,1024]{1,0:T(8,128)} %hid_ref.1, f32[1024,256]{1,0:T(8,128)} %w_ref.1, f32[128,256]{1,0:T(8,128)} %clip_ref.1, s32[1,128]{1,0:T(1,128)} %bitcast.1, f32[1]{0:T(128)S(6)} %copy.11.scale_ref), custom_call_target="tpu_custom_call" | custom-call | tf_op jit(solution)/shard_map/contrastive/pallas_call | solution.py:447
  89.7 0.0 copy-start.1
  89.7 0.0 copy-start
  89.7 1.6 %copy.12 = f32[128,256]{1,0:T(8,128)} copy(f32[128,256]{1,0:T(8,128)} %get-tuple-element.6) | data formatting | bytes 262144
  91.3 0.0 copy-done.1
  91.3 0.6 copy.13
  92.0 0.0 copy-done
  92.0 0.7 copy.14
Async XLA Ops:
  89.7 1.6 %copy-start.1 = (f32[16,256]{1,0:T(8,128)S(1)}, f32[16,256]{1,0:T(8,128)}, u32[]{:S(2)}) copy-start(f32[16,256]{1,0:T(8,128)} %get-tuple-element.7) | copy-start | bytes 49156
  89.7 2.2 %copy-start = (f32[128,256]{1,0:T(8,128)S(1)}, f32[128,256]{1,0:T(8,128)}, u32[]{:S(2)}) copy-start(f32[128,256]{1,0:T(8,128)} %get-tuple-element.8) | copy-start | bytes 393220

commit v2 on v1

v2 whole, which is shorter than its diff:
```python
import math

import jax
import jax.numpy as jnp
from jax import lax
from jax.experimental import pallas as pl
from jax.experimental.pallas import tpu as pltpu
from jax.sharding import PartitionSpec as P

MESH = pl.DeviceIdType.MESH
EPSILON = 1e-06
PRECISE = lax.Precision.HIGHEST
F32 = jnp.float32
BF16 = jnp.bfloat16

COUNT = 136
GROUPS = 8
GROUP_TILES = 1024
TURN = (1, 3)
CAME = (3, 1)
CHUNKS = (2, 1, 3, 0)


def split(value):
    high = value.astype(BF16)
    return high, (value - high.astype(F32)).astype(BF16)


def product(a, b, dims):
    return lax.dot_general(a, b, (dims, ((), ())), preferred_element_type=F32)


def product3(a, b, dims):
    (ah, al), (bh, bl) = a, b
    return product(ah, bh, dims) + product(ah, bl, dims) + product(al, bh, dims)


def exact(a, b, dims):
    return lax.dot_general(a, b, (dims, ((), ())), precision=PRECISE, preferred_element_type=F32)


def turned(column):
    return jnp.broadcast_to(column, (128, 128)).T[0:1, :]


def upright(line):
    return jnp.broadcast_to(line, (128, 128)).T[:, 0:1]


def joined(stats):
    top = stats[0][0]
    for part in stats[1:]:
        top = jnp.maximum(top, part[0])
    total = stats[0][1] * jnp.exp(stats[0][0] - top)
    for part in stats[1:]:
        total = total + part[1] * jnp.exp(part[0] - top)
    return top, total


def kernel(
    hid_hbm, w_hbm, clip_ref, pos_ref, scale_ref,
    gh_ref, gw_ref, gc_ref,
    text, text_h, text_l, clip, clip_h, clip_l, pos, inv_t, scores, exp_r, exp_c, max_t, sum_t,
    row_stat, row_got_y, row_got_x, col_stat, col_got, col_keep, fac_t, g_h, g_l,
    part, part_c, got_aa, got_bb, got_a, got_b, got_ya, got_xb,
    along_own, along_c, along_pair, along_y, along_sum, along_x, cpart, cgot, hpart, hgot, wpart, wgot_c, wgot_x, wgot_z,
    cback, hid_ref, w_ref, blank, ss, rs, ls,
):
    z = lax.axis_index("txt")
    k = lax.axis_index("clip")
    y = lax.axis_index("proj")
    x = k // 2
    c = lax.rem(k, 2)
    o = 1 - c

    def on_z(d):
        return lax.rem(z + d, 8)

    def on_x(d):
        return lax.rem(x + d, 4)

    def on_y(d):
        return lax.rem(y + d, 4)

    partner = (z, 2 * x + o, y)

    def z_peer(d):
        return (on_z(d), k, y)

    def x_peer(d):
        return (z, 2 * on_x(d) + c, y)

    def y_peer(d):
        return (z, k, on_y(d))

    def y_other(d):
        return (z, 2 * x + o, on_y(d))

    groups = [0]
    places = {}

    def slot(key):
        return places.setdefault(key, len(places))

    def copy_of(src, dst, key, device):
        return pltpu.make_async_remote_copy(
            src_ref=src, dst_ref=dst, send_sem=ss.at[len(groups) - 1], recv_sem=rs.at[slot(key)],
            device_id=device, device_id_type=MESH,
        )

    def send(src, dst, key, device):
        tiles = math.prod(src.shape) // 1024
        if groups[-1] + tiles > GROUP_TILES:
            groups.append(0)
        groups[-1] += tiles
        copy_of(src, dst, key, device).start()

    def arrived(place, key):
        copy_of(place, place, key, partner).wait_recv()

    peers = [partner] + [y_peer(d) for d in (1, 2, 3)] + [x_peer(d) for d in (1, 2, 3)]
    peers += [z_peer(d) for d in range(1, 8)] + [y_other(d) for d in (1, 2, 3)]
    barrier = pltpu.get_barrier_semaphore()
    for device in peers:
        pl.semaphore_signal(barrier, inc=1, device_id=device, device_id_type=MESH)
    loads = [
        pltpu.make_async_copy(hid_hbm, hid_ref, ls.at[0]),
        pltpu.make_async_copy(w_hbm, w_ref, ls.at[1]),
    ]
    for load in loads:
        load.start()
    scale = scale_ref[0]
    pos[c, x] = jnp.broadcast_to(pos_ref[...], (8, 128))
    clip[z, y] = clip_ref[pl.ds(pl.multiple_of(y * 32, 32), 32), :]
    for load in loads:
        load.wait()
    text[y, x, c] = exact(hid_ref[...], w_ref[...], ((1,), (0,)))
    pl.semaphore_wait(barrier, len(peers))

    for d in (1, 2, 3):
        rows = pl.ds(pl.multiple_of(on_y(d) * 32, 32), 32)
        send(clip_ref.at[rows], clip.at[z, y], ("clip_y", d), y_peer(d))
    for d in (1, 2, 3):
        send(pos.at[c, x], pos.at[c, x], ("pos_x", d - 1), x_peer(d))

    def rows_of(kind, part=None):
        return pl.ds(64 * kind, 64) if part is None else pl.ds(64 * kind + 32 * part, 32)

    def block_of(kind, near, far, part=None):
        dy, dx = (far, near) if kind == 0 else (near, far)
        return text.at[on_y(dy), on_x(dx), c, rows_of(kind, part)]

    def near_peer(kind, d):
        return x_peer(d) if kind == 0 else y_peer(d)

    def far_peer(kind, d):
        return y_peer(d) if kind == 0 else x_peer(d)

    def spread(block, key, device):
        send(block, block, key, device)

    def begin(kind):
        for way in (0, 1):
            spread(block_of(kind, 0, 0), ("n", kind, way), near_peer(kind, TURN[way]))

    def cross(kind, e):
        for way in (0, 1):
            spread(block_of(kind, e, 0), ("f", kind, e, way), far_peer(kind, TURN[way]))

    def relay_near(kind):
        for way in (0, 1):
            arrived(block_of(kind, CAME[way], 0), ("n", kind, way))
            spread(block_of(kind, CAME[way], 0, way), ("nn", kind), near_peer(kind, TURN[way]))

    def relay_far(kind, e):
        for way in (0, 1):
            arrived(block_of(kind, e, CAME[way]), ("f", kind, e, way))
            spread(block_of(kind, e, CAME[way], way), ("ff", kind), far_peer(kind, TURN[way]))

    def group_of(kind, far, core):
        rows = rows_of(kind)
        return text.at[on_y(far), :, core, rows] if kind == 0 else text.at[:, on_x(far), core, rows]

    def to_partner(kind, far):
        spread(group_of(kind, far, c), ("p", kind, far), partner)

    def clip_piece(far, d):
        return clip.at[on_z(far), on_y(d)]

    def ring_clip(step, d):
        for way in (0, 1):
            if step > 1:
                ring_clip_wait(step - 1, d, way)
            if step < 4 or d in ((0, 3), (1, 2))[way]:
                block = clip_piece(9 - step if way == 0 else step - 1, d)
                spread(block, ("gz", step, d, way), z_peer(1 if way == 0 else 7))

    def ring_clip_wait(step, d, way):
        arrived(clip_piece(8 - step if way == 0 else step, d), ("gz", step, d, way))

    ring_clip(1, 0)
    for kind in (0, 1):
        begin(kind)
    for kind in (0, 1):
        cross(kind, 0)
    for d in (1, 3, 2):
        arrived(clip_piece(0, d), ("clip_y", 4 - d))
        ring_clip(1, d)
    for d in (1, 2, 3):
        arrived(pos.at[c, on_x(4 - d)], ("pos_x", d - 1))
    send(pos.at[c], pos.at[c], ("pos_c", 0), partner)
    ring_clip(2, 0)
    for kind in (0, 1):
        relay_near(kind)
        for e in CAME:
            cross(kind, e)
    for d in (1, 3, 2):
        ring_clip(2, d)
    for kind in (0, 1):
        relay_far(kind, 0)
    ring_clip(3, 0)
    for kind in (0, 1):
        arrived(block_of(kind, 2, 0), ("nn", kind))
        cross(kind, 2)
    for d in (1, 3, 2):
        ring_clip(3, d)
    for kind in (0, 1):
        to_partner(kind, 0)
        for e in CAME:
            relay_far(kind, e)
    ring_clip(4, 0)
    for d in (1, 3, 2):
        ring_clip(4, d)
    for kind in (0, 1):
        relay_far(kind, 2)
        for d in CAME:
            to_partner(kind, d)
    for kind in (0, 1):
        arrived(group_of(kind, 2, c), ("ff", kind))
        to_partner(kind, 2)
    for d in (0, 1, 3, 2):
        ring_clip_wait(4, d, 0 if d in (0, 3) else 1)

    def clip_block(f, squares):
        block = clip[:, f].reshape(256, 256)
        clip_h[f], clip_l[f] = split(block)
        return squares + jnp.sum(block * block, axis=1, keepdims=True)

    inv_c = lax.rsqrt(lax.fori_loop(0, 4, clip_block, jnp.zeros((256, 1), F32)) + EPSILON)
    col_scale = scale * inv_c

    for d in (0, 1, 3, 2):
        for kind in (0, 1):
            arrived(group_of(kind, d, o), ("p", kind, d))
    arrived(pos.at[o], ("pos_c", 0))

    def score(q, carry):
        squares = jnp.zeros((256, 1), F32)
        total = jnp.zeros((256, 256), F32)
        for f in range(4):
            block = text[f, q].reshape(256, 256)
            high, low = split(block)
            text_h[f, q], text_l[f, q] = high, low
            squares = squares + jnp.sum(block * block, axis=1, keepdims=True)
            total = total + product3((clip_h[f], clip_l[f]), (high, low), ((1,), (1,)))
        inverse = lax.rsqrt(squares + EPSILON)
        lanes = jnp.concatenate([turned(inverse[0:128]), turned(inverse[128:256])], axis=1)
        inv_t[q] = jnp.broadcast_to(lanes, (8, 256))
        tile = total * col_scale * lanes
        scores[q] = tile
        top = jnp.max(tile, axis=0, keepdims=True)
        raised = jnp.exp(tile - top)
        exp_r[q] = raised
        max_t[q] = jnp.broadcast_to(top, (8, 256))
        sum_t[q] = jnp.broadcast_to(jnp.sum(raised, axis=0, keepdims=True), (8, 256))
        return carry

    lax.fori_loop(0, 4, score, 0)

    for q in range(4):
        for h in (0, 1):
            row = 2 * q + h
            row_stat[0, row : row + 1, :] = max_t[q, 0:1, h * 128 : h * 128 + 128]
            row_stat[0, 8 + row : 9 + row, :] = sum_t[q, 0:1, h * 128 : h * 128 + 128]
    send(row_stat.at[0], row_got_y.at[0], ("stat",), partner)
    for d in (2, 1, 3):
        send(row_stat.at[0], row_got_y.at[d], ("stat",), y_peer(d))
        send(row_stat.at[0], row_got_y.at[3 + d], ("stat",), y_other(d))
    top_c = jnp.max(scores[0], axis=1, keepdims=True)
    for q in range(1, 4):
        top_c = jnp.maximum(top_c, jnp.max(scores[q], axis=1, keepdims=True))
    total_c = jnp.zeros((256, 1), F32)
    for q in range(4):
        raised = jnp.exp(scores[q] - top_c)
        exp_c[q] = raised
        total_c = total_c + jnp.sum(raised, axis=1, keepdims=True)
    for h in (0, 1):
        col_stat[h : h + 1, :] = turned(top_c[h * 128 : h * 128 + 128])
        col_stat[2 + h : 3 + h, :] = turned(total_c[h * 128 : h * 128 + 128])
    col_stat[4:8, :] = jnp.zeros((4, 128), F32)
    for d in range(1, 8):
        send(col_stat, col_got.at[d - 1], ("stat_z",), z_peer(d))

    def row_part(value):
        return value[0:8], value[8:16]

    arrived(row_got_y, ("stat",))
    stats = joined([row_part(row_stat[0])] + [row_part(row_got_y[d]) for d in range(7)])
    row_stat[2, 0:8], row_stat[2, 8:16] = stats
    for d in (1, 3, 2):
        send(row_stat.at[2], row_got_x.at[d - 1], ("stat_x",), x_peer(d))
    arrived(col_got, ("stat_z",))

    def col_part(value):
        return value[0:2], value[2:4]

    top_g, total_g = joined([col_part(col_stat[...])] + [col_part(col_got[d]) for d in range(7)])
    fac = 0.5 * jnp.exp(col_stat[0:2] - top_g) / total_g
    fac_c = jnp.concatenate([upright(fac[0:1]), upright(fac[1:2])], axis=0)
    arrived(row_got_x, ("stat_x",))
    top_g, total_g = joined([stats] + [row_part(row_got_x[d]) for d in range(3)])
    fac = 0.5 * jnp.exp(row_stat[0, 0:8] - top_g) / total_g
    for q in range(4):
        for h in (0, 1):
            row = 2 * q + h
            fac_t[q, :, h * 128 : h * 128 + 128] = jnp.broadcast_to(fac[row : row + 1], (8, 128))

    number = lax.broadcasted_iota(jnp.int32, (256, 256), 0)
    clip_id = lax.shift_right_logical(number, 5) * 1024 + (number & 31) + (k * 128 + y * 32)

    def gradient(i):
        q = on_x(CHUNKS[i])
        target = jnp.concatenate([pos[0, q, 0:1, :], pos[1, q, 0:1, :]], axis=1)
        grad = exp_r[q] * fac_t[q, 0:1, :] + exp_c[q] * fac_c
        grad = grad - (clip_id == target).astype(F32)
        line = jnp.sum(grad * scores[q], axis=0, keepdims=True)
        for h in (0, 1):
            along_own[2 * i + h : 2 * i + h + 1, :] = line[:, h * 128 : h * 128 + 128]
        g_h[q], g_l[q] = split(grad * (scale * inv_t[q, 0:1, :]))
        weighted = split(grad * col_scale)
        for f in range(4):
            block = product3(weighted, (clip_h[f], clip_l[f]), ((0,), (0,)))
            part[f, q] = block.reshape(2, 128, 256)
        send(part.at[:, q, o], part_c.at[:, q], ("rc", i), partner)

    for i in range(4):
        gradient(i)
    send(along_own, along_c, ("along_c", 0), partner)

    def clip_gradient(f, carry):
        total = jnp.zeros((256, 256), F32)
        for q in range(4):
            total = total + product3((g_h[q], g_l[q]), (text_h[f, q], text_l[f, q]), ((1,), (0,)))
        cpart[:, f] = total.reshape(8, 32, 256)
        return carry

    lax.fori_loop(0, 4, clip_gradient, 0)

    def ring_sum(step):
        for f in range(4):
            for way in (0, 1):
                goal = on_z(5 - step) if way == 0 else on_z(3 + step)
                if step > 2 or (step == 2 and f // 2 == way):
                    place = cgot.at[way, step - 2, f]
                    arrived(place, ("cz", step - 1, f, way))
                    cpart[goal, f] = cpart[goal, f] + place[...]
                if step > 1 or f // 2 == way:
                    send(
                        cpart.at[goal, f], cgot.at[way, step - 1, f],
                        ("cz", step, f if step < 4 else 0, way), z_peer(1 if way == 0 else 7),
                    )

    def half_of(part):
        return pl.ds(32 * part, 32)

    def pass_a(d, way, half):
        send(
            part.at[:, on_x(d), c, rows_of(0, half)], got_a.at[way, :, half_of(half)],
            ("ra", way), x_peer(TURN[way]),
        )

    def pass_b(i, d, way, half):
        send(
            part.at[on_y(d), on_x(CHUNKS[i]), c, rows_of(1, half)], got_b.at[way, i, half_of(half)],
            ("rb", i, way), y_peer(TURN[way]),
        )

    def join_cores(i):
        q = on_x(CHUNKS[i])
        arrived(part_c.at[:, q], ("rc", i))
        for f in range(4):
            part[f, q, c] = part[f, q, c] + part_c[f, q]
        for way in (0, 1):
            if i == 0:
                send(
                    part.at[:, q, c, rows_of(0, way)], got_aa.at[way], ("raa", way), x_peer(TURN[way])
                )
            if CHUNKS[i] == TURN[way]:
                pass_a(TURN[way], way, 1 - way)
            send(
                part.at[on_y(2), q, c, rows_of(1, way)], got_bb.at[way, i], ("rbb", i, way),
                y_peer(TURN[way]),
            )
        for way in (0, 1):
            pass_b(i, TURN[way], way, 1 - way)

    def relay_a():
        for way in (0, 1):
            arrived(got_aa.at[way], ("raa", way))
            at = slice(32 * way, 32 * way + 32)
            for f in range(4):
                part[f, on_x(TURN[way]), c, at] = part[f, on_x(TURN[way]), c, at] + got_aa[way, f]
            pass_a(TURN[way], way, way)

    def relay_b(i):
        q = on_x(CHUNKS[i])
        for way in (0, 1):
            arrived(got_bb.at[way, i], ("rbb", i, way))
            at = slice(64 + 32 * way, 96 + 32 * way)
            part[on_y(TURN[way]), q, c, at] = part[on_y(TURN[way]), q, c, at] + got_bb[way, i]
            pass_b(i, TURN[way], way, way)

    def finish_a():
        for way in (0, 1):
            arrived(got_a.at[way], ("ra", way))
        for d in (2, 1, 3, 0):
            e = on_y(d)
            part[e, x, c, 0:64] = part[e, x, c, 0:64] + got_a[0, e] + got_a[1, e]
            if d > 0:
                send(part.at[e, x, c, rows_of(0)], got_ya.at[d - 1], ("ya",), y_peer(d))

    def finish_b(i):
        q = on_x(CHUNKS[i])
        for way in (0, 1):
            arrived(got_b.at[way, i], ("rb", i, way))
        part[y, q, c, 64:128] = part[y, q, c, 64:128] + got_b[0, i] + got_b[1, i]
        d = CHUNKS[i]
        if d > 0:
            send(part.at[y, q, c, rows_of(1)], got_xb.at[d - 1], ("xb",), x_peer(d))

    join_cores(0)
    ring_sum(1)
    join_cores(1)
    join_cores(2)
    join_cores(3)
    arrived(along_c, ("along_c", 0))
    along_pair[...] = along_own[...] + along_c[...]
    for d in (2, 1, 3):
        send(along_pair, along_y.at[d - 1], ("along_y",), y_peer(d))
    relay_a()
    relay_b(0)
    ring_sum(2)
    relay_b(1)
    relay_b(2)
    arrived(along_y, ("along_y",))
    along_sum[...] = along_pair[...] + along_y[0] + along_y[1] + along_y[2]
    for d in (2, 1, 3):
        send(along_sum, along_x.at[d - 1], ("along_x",), x_peer(d))
    relay_b(3)
    ring_sum(3)
    finish_b(0)
    finish_a()
    for i in (1, 2, 3):
        finish_b(i)
    ring_sum(4)

    for way in (0, 1):
        arrived(cgot.at[way, 3], ("cz", 4, 0, way))
    squares = jnp.zeros((32, 1), F32)
    along = jnp.zeros((32, 1), F32)
    for f in range(4):
        total = cpart[z, f] + cgot[0, 3, f] + cgot[1, 3, f]
        raw = clip[z, f]
        cback[f] = total
        squares = squares + jnp.sum(raw * raw, axis=1, keepdims=True)
        along = along + jnp.sum(raw * total, axis=1, keepdims=True)
    inverse = lax.rsqrt(squares + EPSILON)
    for f in range(4):
        cback[f] = (cback[f] - (clip[z, f] * inverse) * (along * inverse)) * inverse
    for d in (1, 3, 2):
        send(cback.at[on_y(d)], col_keep.at[d - 1], ("gc",), y_peer(d))

    squares = jnp.zeros((128, 1), F32)
    for f in range(4):
        raw = text[f, x, c]
        squares = squares + jnp.sum(raw * raw, axis=1, keepdims=True)
    inverse = lax.rsqrt(squares + EPSILON)
    arrived(got_ya, ("ya",))
    arrived(got_xb, ("xb",))
    arrived(along_x, ("along_x",))
    lines = along_sum[6:8]
    for d in (1, 2, 3):
        at = 2 * CHUNKS.index(d)
        lines = lines + along_x[d - 1, at : at + 2]
    along = upright(jnp.where(c == 0, lines[0:1], lines[1:2]))
    upper = part[y, x, c, 0:64] + got_ya[0] + got_ya[1] + got_ya[2]
    lower = part[y, x, c, 64:128] + got_xb[0] + got_xb[1] + got_xb[2]
    cot = jnp.concatenate([upper, lower], axis=0)
    back = (cot - (text[y, x, c] * inverse) * along) * inverse

    order = (4, 3, 5, 2, 6, 1, 7, 0)

    def weight(t):
        for j in range(4 * t, 4 * t + 4):
            rows = pl.ds(pl.multiple_of(on_z(order[j]) * 128, 128), 128)
            wpart[j] = exact(hid_ref[:, rows], back, ((0,), (0,))).reshape(4, 2, 16, 256)
        send(wpart.at[4 * t : 4 * t + 4, :, o], wgot_c.at[4 * t : 4 * t + 4], ("wc", t), partner)

    def hidden(d):
        rows = pl.ds(pl.multiple_of(on_y(d) * 256, 256), 256)
        hpart[d] = exact(back, w_ref[rows, :], ((1,), (1,)))
        if d > 0:
            send(hpart.at[d], hgot.at[d - 1], ("hid",), y_peer(d))

    def weight_x(t):
        arrived(wgot_c.at[4 * t : 4 * t + 4], ("wc", t))
        for j in range(4 * t, 4 * t + 4):
            for f in range(4):
                wpart[j, f, c] = wpart[j, f, c] + wgot_c[j, f]
        for d in (2, 1, 3):
            send(
                wpart.at[4 * t : 4 * t + 4, on_x(d), c], wgot_x.at[d - 1, 4 * t : 4 * t + 4],
                ("wx", t), x_peer(d),
            )

    def weight_z(t):
        arrived(wgot_x.at[:, 4 * t : 4 * t + 4], ("wx", t))
        for j in range(4 * t, 4 * t + 4):
            wpart[j, x, c] = wpart[j, x, c] + wgot_x[0, j] + wgot_x[1, j] + wgot_x[2, j]
            d = order[j]
            if d > 0:
                send(wpart.at[j, x, c], wgot_z.at[d - 1], ("wz",), z_peer(d))

    weight(0)
    hidden(2)
    weight(1)
    weight_x(0)
    hidden(1)
    hidden(3)
    weight_x(1)
    hidden(0)
    weight_z(0)
    gc_ref[pl.ds(pl.multiple_of(y * 32, 32), 32), :] = cback[y]
    arrived(col_keep, ("gc",))
    for d in (1, 2, 3):
        gc_ref[pl.ds(pl.multiple_of(on_y(4 - d) * 32, 32), 32), :] = col_keep[d - 1]
    weight_z(1)
    arrived(hgot, ("hid",))
    gh_ref[...] = hpart[0] + hgot[0] + hgot[1] + hgot[2]
    total = wpart[7, x, c]
    arrived(wgot_z, ("wz",))
    for d in order[:7]:
        total = total + wgot_z[d - 1]
    gw_ref[...] = total
    for group, tiles in enumerate(groups):
        whole = blank.at[pl.ds(0, tiles)]
        pltpu.make_async_remote_copy(
            src_ref=whole, dst_ref=whole, send_sem=ss.at[group], recv_sem=rs.at[0],
            device_id=partner, device_id_type=MESH,
        ).wait_send()


def body(text_hidden, proj_weight, clip_embed, positive, logit_scale):
    whole = pl.BlockSpec(memory_space=pl.ANY)
    vmem = pl.BlockSpec(memory_space=pltpu.VMEM)
    scratch = [
        ((4, 4, 2, 128, 256), F32), ((4, 4, 256, 256), BF16), ((4, 4, 256, 256), BF16),
        ((8, 4, 32, 256), F32), ((4, 256, 256), BF16), ((4, 256, 256), BF16),
        ((2, 4, 8, 128), jnp.int32), ((4, 8, 256), F32),
        ((4, 256, 256), F32), ((4, 256, 256), F32), ((4, 256, 256), F32), ((4, 8, 256), F32), ((4, 8, 256), F32),
        ((3, 16, 128), F32), ((7, 16, 128), F32), ((3, 16, 128), F32),
        ((8, 128), F32), ((7, 8, 128), F32), ((3, 32, 256), F32), ((4, 8, 256), F32),
        ((4, 256, 256), BF16), ((4, 256, 256), BF16),
        ((4, 4, 2, 128, 256), F32), ((4, 4, 128, 256), F32),
        ((2, 4, 32, 256), F32), ((2, 4, 32, 256), F32), ((2, 4, 64, 256), F32), ((2, 4, 64, 256), F32),
        ((3, 64, 256), F32), ((3, 64, 256), F32),
        ((8, 128), F32), ((8, 128), F32), ((8, 128), F32), ((3, 8, 128), F32), ((8, 128), F32), ((3, 8, 128), F32),
        ((8, 4, 32, 256), F32), ((2, 4, 4, 32, 256), F32),
        ((4, 128, 256), F32), ((3, 128, 256), F32),
        ((8, 4, 2, 16, 256), F32), ((8, 4, 16, 256), F32), ((3, 8, 16, 256), F32), ((7, 16, 256), F32),
        ((4, 32, 256), F32), ((128, 1024), F32), ((1024, 256), F32), ((GROUP_TILES, 8, 128), F32),
    ]
    return pl.pallas_call(
        kernel,
        out_shape=(
            pltpu.VMEM((128, 256), F32),
            pltpu.VMEM((16, 256), F32),
            pltpu.VMEM((128, 256), F32),
        ),
        in_specs=[whole, whole, vmem, vmem, pl.BlockSpec(memory_space=pltpu.SMEM)],
        out_specs=(vmem, vmem, vmem),
        scratch_shapes=[pltpu.VMEM(shape, dtype) for shape, dtype in scratch]
        + [pltpu.SemaphoreType.DMA((n,)) for n in (GROUPS, COUNT, 2)],
        compiler_params=pltpu.CompilerParams(
            collective_id=0, has_side_effects=True, vmem_limit_bytes=56 << 20
        ),
        name="contrastive",
    )(text_hidden, proj_weight, clip_embed, positive.reshape(1, 128), logit_scale)


def solution(mesh):
    rows = ("txt", "clip")
    in_specs = (P(rows, None), P(None, "proj"), P(rows, "proj"), P(rows), P())
    out_specs = (P(rows, "proj"), P(rows, "proj"), P(rows, "proj"))
    return jax.shard_map(body, mesh=mesh, in_specs=in_specs, out_specs=out_specs, check_vma=False)
```

time: 92.8 us -> 83 us (0.89)
  Pallas kernels: 88.4 us -> 79.7 us
  local copies, waits for them, and re-layouts: 2.87 us -> 1.92 us
    pallas_call x1, Pallas kernels: 88.4 us -> 79.7 us  [body(): pl.pallas_call(kernel, out_shape=(pltpu.VMEM((128, 256), F32), pltpu.VMEM...]
    unnamed x7 -> x3, local copies, waits for them, and re-layouts: 2.87 us -> 1.92 us
where the time goes in v2:
time: 83 us; the launch traced here: 82.9 us
  Pallas kernels  79.7 us (96%)
  local copies, waits for them, and re-layouts  1.92 us (2%)
  between operations  1.29 us (2%)
    pallas_call x1, Pallas kernels, body(): pl.pallas_call(kernel, out_shape=(pltpu.VMEM((128, 256), F32), pltpu.VMEM...  79.7 us
    unnamed x3, local copies, waits for them, and re-layouts  1.92 us

profile of v2, /device:TPU:1, one launch (start us, length us, event | category | flops | bytes accessed | tf_op | source)
XLA Modules:
  0.0 82.9 jit_solution(14998025292378274666)
XLA Ops:
  1.3 79.7 %contrastive.1 = (f32[128,256]{1,0:T(8,128)S(1)}, f32[16,256]{1,0:T(8,128)S(1)}, f32[128,256]{1,0:T(8,128)S(1)}) custom-call(f32[128,1024]{1,0:T(8,128)} %hid_hbm.1, f32[1024,256]{1,0:T(8,128)} %w_hbm.1, f32[128,256]{1,0:T(8,128)} %clip_ref.1, s32[1,128]{1,0:T(1,128)} %bitcast.1, f32[1]{0:T(128)S(6)} %copy.14.scale_ref), custom_call_target="tpu_custom_call" | custom-call | tf_op jit(solution)/shard_map/contrastive/pallas_call | solution.py:583
  80.9 0.7 copy.11
  81.6 0.6 copy.12
  82.2 0.7 copy.13

commit v3 on v2

--- a/solution.py
+++ b/solution.py
@@ -13,8 +13,8 @@
 F32 = jnp.float32
 BF16 = jnp.bfloat16
 
-COUNT = 136
-GROUPS = 8
+COUNT = 134
+GROUPS = 3
 GROUP_TILES = 1024
 TURN = (1, 3)
 CAME = (3, 1)
@@ -64,7 +64,7 @@
     row_stat, row_got_y, row_got_x, col_stat, col_got, col_keep, fac_t, g_h, g_l,
     part, part_c, got_aa, got_bb, got_a, got_b, got_ya, got_xb,
     along_own, along_c, along_pair, along_y, along_sum, along_x, cpart, cgot, hpart, hgot, wpart, wgot_c, wgot_x, wgot_z,
-    cback, hid_ref, w_ref, blank, ss, rs, ls,
+    cback, hid_ref, w_ref, hid_h, hid_l, w_h, w_l, blank, ss, rs, ls,
 ):
     z = lax.axis_index("txt")
     k = lax.axis_index("clip")
@@ -135,6 +135,8 @@
     for load in loads:
         load.wait()
     text[y, x, c] = exact(hid_ref[...], w_ref[...], ((1,), (0,)))
+    hid_h[...], hid_l[...] = split(hid_ref[...])
+    w_h[...], w_l[...] = split(w_ref[...])
     pl.semaphore_wait(barrier, len(peers))
 
     for d in (1, 2, 3):
@@ -175,7 +177,10 @@
     def relay_far(kind, e):
         for way in (0, 1):
             arrived(block_of(kind, e, CAME[way]), ("f", kind, e, way))
-            spread(block_of(kind, e, CAME[way], way), ("ff", kind), far_peer(kind, TURN[way]))
+            spread(block_of(kind, e, CAME[way], way), ("ff", kind, e), far_peer(kind, TURN[way]))
+
+    def last_piece(kind, e, core):
+        return text.at[on_y(2), on_x(e), core, rows_of(0)] if kind == 0 else text.at[on_y(e), on_x(2), core, rows_of(1)]
 
     def group_of(kind, far, core):
         rows = rows_of(kind)
@@ -235,9 +240,10 @@
         relay_far(kind, 2)
         for d in CAME:
             to_partner(kind, d)
-    for kind in (0, 1):
-        arrived(group_of(kind, 2, c), ("ff", kind))
-        to_partner(kind, 2)
+    for e in (0, 1, 3, 2):
+        for kind in (0, 1):
+            arrived(last_piece(kind, e, c), ("ff", kind, e))
+            spread(last_piece(kind, e, c), ("q", kind), partner)
     for d in (0, 1, 3, 2):
         ring_clip_wait(4, d, 0 if d in (0, 3) else 1)
 
@@ -251,7 +257,7 @@
 
     for d in (0, 1, 3, 2):
         for kind in (0, 1):
-            arrived(group_of(kind, d, o), ("p", kind, d))
+            arrived(group_of(kind, d, o), ("p", kind, d) if d != 2 else ("q", kind))
     arrived(pos.at[o], ("pos_c", 0))
 
     def score(q, carry):
@@ -464,21 +470,22 @@
         finish_b(i)
     ring_sum(4)
 
-    for way in (0, 1):
-        arrived(cgot.at[way, 3], ("cz", 4, 0, way))
-    squares = jnp.zeros((32, 1), F32)
-    along = jnp.zeros((32, 1), F32)
-    for f in range(4):
-        total = cpart[z, f] + cgot[0, 3, f] + cgot[1, 3, f]
-        raw = clip[z, f]
-        cback[f] = total
-        squares = squares + jnp.sum(raw * raw, axis=1, keepdims=True)
-        along = along + jnp.sum(raw * total, axis=1, keepdims=True)
-    inverse = lax.rsqrt(squares + EPSILON)
-    for f in range(4):
-        cback[f] = (cback[f] - (clip[z, f] * inverse) * (along * inverse)) * inverse
-    for d in (1, 3, 2):
-        send(cback.at[on_y(d)], col_keep.at[d - 1], ("gc",), y_peer(d))
+    def clip_rows():
+        for way in (0, 1):
+            arrived(cgot.at[way, 3], ("cz", 4, 0, way))
+        squares = jnp.zeros((32, 1), F32)
+        along = jnp.zeros((32, 1), F32)
+        for f in range(4):
+            total = cpart[z, f] + cgot[0, 3, f] + cgot[1, 3, f]
+            raw = clip[z, f]
+            cback[f] = total
+            squares = squares + jnp.sum(raw * raw, axis=1, keepdims=True)
+            along = along + jnp.sum(raw * total, axis=1, keepdims=True)
+        inverse = lax.rsqrt(squares + EPSILON)
+        for f in range(4):
+            cback[f] = (cback[f] - (clip[z, f] * inverse) * (along * inverse)) * inverse
+        for d in (1, 3, 2):
+            send(cback.at[on_y(d)], col_keep.at[d - 1], ("gc",), y_peer(d))
 
     squares = jnp.zeros((128, 1), F32)
     for f in range(4):
@@ -499,16 +506,18 @@
     back = (cot - (text[y, x, c] * inverse) * along) * inverse
 
     order = (4, 3, 5, 2, 6, 1, 7, 0)
+    back_parts = split(back)
 
     def weight(t):
         for j in range(4 * t, 4 * t + 4):
             rows = pl.ds(pl.multiple_of(on_z(order[j]) * 128, 128), 128)
-            wpart[j] = exact(hid_ref[:, rows], back, ((0,), (0,))).reshape(4, 2, 16, 256)
+            block = product3((hid_h[:, rows], hid_l[:, rows]), back_parts, ((0,), (0,)))
+            wpart[j] = block.reshape(4, 2, 16, 256)
         send(wpart.at[4 * t : 4 * t + 4, :, o], wgot_c.at[4 * t : 4 * t + 4], ("wc", t), partner)
 
     def hidden(d):
         rows = pl.ds(pl.multiple_of(on_y(d) * 256, 256), 256)
-        hpart[d] = exact(back, w_ref[rows, :], ((1,), (1,)))
+        hpart[d] = product3(back_parts, (w_h[rows, :], w_l[rows, :]), ((1,), (1,)))
         if d > 0:
             send(hpart.at[d], hgot.at[d - 1], ("hid",), y_peer(d))
 
@@ -538,6 +547,7 @@
     hidden(1)
     hidden(3)
     weight_x(1)
+    clip_rows()
     hidden(0)
     weight_z(0)
     gc_ref[pl.ds(pl.multiple_of(y * 32, 32), 32), :] = cback[y]
@@ -578,7 +588,8 @@
         ((8, 4, 32, 256), F32), ((2, 4, 4, 32, 256), F32),
         ((4, 128, 256), F32), ((3, 128, 256), F32),
         ((8, 4, 2, 16, 256), F32), ((8, 4, 16, 256), F32), ((3, 8, 16, 256), F32), ((7, 16, 256), F32),
-        ((4, 32, 256), F32), ((128, 1024), F32), ((1024, 256), F32), ((GROUP_TILES, 8, 128), F32),
+        ((4, 32, 256), F32), ((128, 1024), F32), ((1024, 256), F32),
+        ((128, 1024), BF16), ((128, 1024), BF16), ((1024, 256), BF16), ((1024, 256), BF16), ((GROUP_TILES, 8, 128), F32),
     ]
     return pl.pallas_call(
         kernel,

time: 83 us -> 80.3 us (0.967)
  Pallas kernels: 79.7 us -> 77 us
    pallas_call x1, Pallas kernels: 79.7 us -> 77 us  [body(): pl.pallas_call(kernel, out_shape=(pltpu.VMEM((128, 256), F32), pltpu.VMEM...]
where the time goes in v3:
time: 80.3 us; the launch traced here: 80.2 us
  Pallas kernels  77 us (96%)
  local copies, waits for them, and re-layouts  1.92 us (2%)
  between operations  1.29 us (2%)
    pallas_call x1, Pallas kernels, body(): pl.pallas_call(kernel, out_shape=(pltpu.VMEM((128, 256), F32), pltpu.VMEM...  77 us
    unnamed x3, local copies, waits for them, and re-layouts  1.92 us

profile of v3, /device:TPU:1, one launch (start us, length us, event | category | flops | bytes accessed | tf_op | source)
XLA Modules:
  0.0 80.2 jit_solution(10992316039732410132)
XLA Ops:
  1.3 77.0 %contrastive.1 = (f32[128,256]{1,0:T(8,128)S(1)}, f32[16,256]{1,0:T(8,128)S(1)}, f32[128,256]{1,0:T(8,128)S(1)}) custom-call(f32[128,1024]{1,0:T(8,128)} %hid_hbm.1, f32[1024,256]{1,0:T(8,128)} %w_hbm.1, f32[128,256]{1,0:T(8,128)} %clip_ref.1, s32[1,128]{1,0:T(1,128)} %bitcast.1, f32[1]{0:T(128)S(6)} %copy.14.scale_ref), custom_call_target="tpu_custom_call" | custom-call | tf_op jit(solution)/shard_map/contrastive/pallas_call | solution.py:594
  78.3 0.7 copy.11
  78.9 0.6 copy.12
  79.6 0.7 copy.13

commit v4 on v3

--- a/solution.py
+++ b/solution.py
@@ -164,6 +164,7 @@
     def begin(kind):
         for way in (0, 1):
             spread(block_of(kind, 0, 0), ("n", kind, way), near_peer(kind, TURN[way]))
+        spread(block_of(kind, 0, 0), ("nn", kind), near_peer(kind, 2))
 
     def cross(kind, e):
         for way in (0, 1):
@@ -172,7 +173,6 @@
     def relay_near(kind):
         for way in (0, 1):
             arrived(block_of(kind, CAME[way], 0), ("n", kind, way))
-            spread(block_of(kind, CAME[way], 0, way), ("nn", kind), near_peer(kind, TURN[way]))
 
     def relay_far(kind, e):
         for way in (0, 1):

time: 80.3 us -> 80.4 us (level)
  no operation moved by 1% of the time
where the time goes in v4:
time: 80.4 us; the launch traced here: 80.3 us
  Pallas kernels  77.1 us (96%)
  local copies, waits for them, and re-layouts  1.92 us (2%)
  between operations  1.29 us (2%)
    pallas_call x1, Pallas kernels, body(): pl.pallas_call(kernel, out_shape=(pltpu.VMEM((128, 256), F32), pltpu.VMEM...  77.1 us
    unnamed x3, local copies, waits for them, and re-layouts  1.92 us

profile of v4, /device:TPU:1, one launch (start us, length us, event | category | flops | bytes accessed | tf_op | source)
XLA Modules:
  0.0 80.3 jit_solution(4456754614096209957)
XLA Ops:
  1.3 77.1 %contrastive.1 = (f32[128,256]{1,0:T(8,128)S(1)}, f32[16,256]{1,0:T(8,128)S(1)}, f32[128,256]{1,0:T(8,128)S(1)}) custom-call(f32[128,1024]{1,0:T(8,128)} %hid_hbm.1, f32[1024,256]{1,0:T(8,128)} %w_hbm.1, f32[128,256]{1,0:T(8,128)} %clip_ref.1, s32[1,128]{1,0:T(1,128)} %bitcast.1, f32[1]{0:T(128)S(6)} %copy.14.scale_ref), custom_call_target="tpu_custom_call" | custom-call | tf_op jit(solution)/shard_map/contrastive/pallas_call | solution.py:594
  78.4 0.7 copy.11
  79.1 0.6 copy.12
  79.7 0.7 copy.13
